TPU v7x, 32 devices: a whole 2x2x4 slice. The times are simulated.
32 devices in a mesh: expert: 4 (over z), ctx: 4 (over x, core), dp: 2 (over y).
Axes of the slice: x: 2, y: 2, z: 4, core: 2. Of those that a mesh axis runs over, the one named last changes fastest.
Arguments:
- inputs: bfloat16 [4, 1024, 768], P('expert', ('ctx', 'dp')), may hold values from -6 to 6
- cotangent: bfloat16 [4, 1024, 768], P('expert', ('ctx', 'dp')), may hold values from -6 to 6
- expert_ids: int32 [4, 1024, 2], P('expert', ('ctx', 'dp')), may hold values from 0 to 3, all different within a row; in each aligned block of 128 rows (0 to 127, 128 to 255, ..., all dimensions but the last counted through in order) at most 72 rows name the same one
- first_gain: float32 [768], replicated, may hold values from 0.1 to 1.9
- query_weight: bfloat16 [768, 768], replicated, may hold values from -0.21875 to 0.21875
- key_weight: bfloat16 [768, 768], replicated, may hold values from -0.21875 to 0.21875
- value_weight: bfloat16 [768, 768], replicated, may hold values from -0.21875 to 0.21875
- merge_weight: bfloat16 [768, 768], replicated, may hold values from -0.875 to 0.875
- relative_bucket_bias: float32 [32, 12], replicated, may hold values from -4 to 4
- expert_norm_gain: float32 [768], replicated, may hold values from 0.1 to 1.9
- router_weight: bfloat16 [768, 4], replicated, may hold values from -0.15625 to 0.15625
- gate_weight: bfloat16 [4, 768, 3072], P('expert', None, 'ctx'), may hold values from -0.21875 to 0.21875
- up_weight: bfloat16 [4, 768, 3072], P('expert', None, 'ctx'), may hold values from -0.21875 to 0.21875
- down_weight: bfloat16 [4, 3072, 768], P('expert', 'ctx'), may hold values from -0.109375 to 0.109375
Outputs:
- layer_output: bfloat16 [4, 1024, 768], P('expert', ('ctx', 'dp'))
- input_grad: float32 [4, 1024, 768], P('expert', ('ctx', 'dp'))
- first_grad: float32 [768], replicated
- query_grad: float32 [768, 768], P(('ctx', 'dp'), 'expert')
- key_grad: float32 [768, 768], P(('ctx', 'dp'), 'expert')
- value_grad: float32 [768, 768], P(('ctx', 'dp'), 'expert')
- merge_grad: float32 [768, 768], P(('ctx', 'dp'), 'expert')
- bias_grad: float32 [32, 12], replicated
- second_grad: float32 [768], replicated
- router_grad: float32 [768, 4], replicated
- gate_grad: float32 [4, 768, 3072], P('expert', 'dp', 'ctx')
- up_grad: float32 [4, 768, 3072], P('expert', 'dp', 'ctx')
- down_grad: float32 [4, 3072, 768], P('expert', 'ctx', 'dp')
Inputs may be any that keep to these rules, and one draw needn't show every extreme that they name: `expert_ids`: A token's two experts differ. In each sequence, the 128 positions of an aligned block name any one expert at most 72 times, and in every draw some expert is named exactly 72 times in some block.
All inputs are finite; a program needn't handle non-finite values.
Results may differ from a plain program's by a relative error of at most 0.017.
Values may be sent and summed in bfloat16 or wider, within the bound.
A program may use at most 192 MiB of HBM per device.

v0:
```python
import math

import jax
import jax.numpy as jnp
from jax import lax
from jax.sharding import PartitionSpec as P

norm_eps = 1e-06
reach_span = 128.0


def bucket_bounds(bucket_num):
    exact_span = bucket_num // 2
    bounds = list(range(1, exact_span))
    for target in range(exact_span, bucket_num):
        border = exact_span
        while (
            exact_span
            + int(math.log(border / exact_span) / math.log(reach_span / exact_span) * exact_span)
            < target
        ):
            border += 1
        bounds.append(border)
    return bounds


def distance_buckets(distance, bucket_num):
    counted = jnp.zeros(distance.shape, jnp.int32)
    for border in bucket_bounds(bucket_num):
        counted = counted + (distance >= border).astype(jnp.int32)
    return counted


def rms_scale(values, gain_vec):
    return (
        values * lax.rsqrt(jnp.mean(values * values, axis=-1, keepdims=True) + norm_eps) * gain_vec
    )


def gated_hidden(gate_pre, up_pre):
    return jax.nn.gelu(gate_pre, approximate=False) * up_pre


def pair_softmax(logit_pair):
    return jax.nn.softmax(logit_pair, axis=-1)


def bucket_table(distance, bucket_num):
    bucket_of = distance_buckets(distance, bucket_num)
    return (lax.iota(jnp.int32, bucket_num)[:, None, None] == bucket_of[None]).astype(jnp.float32)


def per_device(
    inputs,
    cotangent,
    expert_ids,
    first_gain,
    query_weight,
    key_weight,
    value_weight,
    merge_weight,
    relative_bucket_bias,
    expert_norm_gain,
    router_weight,
    gate_weight,
    up_weight,
    down_weight,
):
    seq_count, pos_count, model_width = inputs.shape
    tok_count = seq_count * pos_count
    bucket_num, heads_num = relative_bucket_bias.shape
    head_dimension = model_width // heads_num
    score_scale = head_dimension ** (-0.5)
    expert_num = router_weight.shape[1]
    local_experts = gate_weight.shape[0]
    owners = lax.axis_size("expert")
    places = lax.axis_size(("ctx", "dp"))
    seq_len = pos_count * places
    capacity = min(pos_count, max(2, 9 * pos_count // (4 * expert_num)))
    lane_rows = seq_count * capacity
    buffer_rows = expert_num * lane_rows
    highest_precision = lax.Precision.HIGHEST
    residual = inputs.astype(jnp.float32)
    first_normed, first_back = jax.vjp(rms_scale, residual, first_gain)
    mixer_in = first_normed.astype(jnp.bfloat16)
    queries = jnp.einsum(
        "spd,de->spe", mixer_in, query_weight, preferred_element_type=jnp.float32
    ).astype(jnp.bfloat16)
    keys_local = jnp.einsum(
        "spd,de->spe", mixer_in, key_weight, preferred_element_type=jnp.float32
    ).astype(jnp.bfloat16)
    values_local = jnp.einsum(
        "spd,de->spe", mixer_in, value_weight, preferred_element_type=jnp.float32
    ).astype(jnp.bfloat16)
    keys_whole, values_whole = (
        lax.all_gather(keys_local, ("ctx", "dp"), axis=1, tiled=True),
        lax.all_gather(values_local, ("ctx", "dp"), axis=1, tiled=True),
    )
    query_heads = queries.reshape(seq_count, pos_count, heads_num, head_dimension)
    key_heads = keys_whole.reshape(seq_count, seq_len, heads_num, head_dimension)
    value_heads = values_whole.reshape(seq_count, seq_len, heads_num, head_dimension)
    first_pos = lax.axis_index(("ctx", "dp")) * pos_count
    query_pos = first_pos + lax.iota(jnp.int32, pos_count)
    offsets = query_pos[:, None] - lax.iota(jnp.int32, seq_len)[None, :]
    visible = offsets >= 0
    distance = jnp.clip(offsets, 0, seq_len - 1)
    bucket_onehot = bucket_table(distance, bucket_num)
    bias_lattice = jnp.einsum(
        "ry,rta->yta", relative_bucket_bias, bucket_onehot, precision=highest_precision
    )

    def score_grid():
        raw_scores = (
            jnp.einsum(
                "sqhd,skhd->shqk", query_heads, key_heads, preferred_element_type=jnp.float32
            )
            * score_scale
            + bias_lattice[None]
        )
        return jnp.where(visible[None, None], raw_scores, -1e30)

    masked = score_grid()
    row_top = jnp.max(masked, axis=-1, keepdims=True)
    exp_terms = jnp.exp(masked - row_top)
    row_total = jnp.sum(exp_terms, axis=-1, keepdims=True)
    prob_mass = exp_terms / row_total
    log_total = row_top + jnp.log(row_total)
    attended = jnp.einsum(
        "shqk,skhd->sqhd",
        prob_mass.astype(jnp.bfloat16),
        value_heads,
        preferred_element_type=jnp.float32,
    )
    mixed_heads = attended.reshape(seq_count, pos_count, model_width).astype(jnp.bfloat16)
    hidden_state = residual + jnp.einsum(
        "spd,de->spe", mixed_heads, merge_weight, preferred_element_type=jnp.float32
    )
    second_normed, second_back = jax.vjp(rms_scale, hidden_state, expert_norm_gain)
    expert_input = second_normed.astype(jnp.bfloat16).reshape(tok_count, model_width)
    logits = jnp.einsum(
        "td,de->te", expert_input, router_weight, preferred_element_type=jnp.float32
    )
    routed_ids = expert_ids.reshape(tok_count, 2)
    picked_logits = jnp.take_along_axis(logits, routed_ids, axis=1)
    gate_values, gate_back = jax.vjp(pair_softmax, picked_logits)
    assign_ids = expert_ids.reshape(seq_count, pos_count * 2)
    expert_hot = (assign_ids[:, :, None] == lax.iota(jnp.int32, expert_num)[None, None, :]).astype(
        jnp.int32
    )
    earlier = jnp.cumsum(expert_hot, axis=1) - expert_hot
    slot_pos = jnp.sum(earlier * expert_hot, axis=-1).astype(jnp.int32)
    target = assign_ids * lane_rows + lax.iota(jnp.int32, seq_count)[:, None] * capacity + slot_pos
    target_flat = target.reshape(tok_count * 2)
    slot_hits = target_flat[None, :] == lax.iota(jnp.int32, buffer_rows)[:, None]
    assign_index = lax.iota(jnp.int32, tok_count * 2)[None, :]
    slot_source = jnp.where(
        jnp.any(slot_hits, axis=1),
        jnp.sum(jnp.where(slot_hits, assign_index, 0), axis=1),
        tok_count * 2,
    ).astype(jnp.int32)
    padded_in = jnp.concatenate([expert_input, jnp.zeros((1, model_width), jnp.bfloat16)], axis=0)
    dispatched = jnp.take(padded_in, slot_source // 2, axis=0).reshape(
        owners, local_experts, lane_rows, model_width
    )
    arrived = lax.all_to_all(dispatched, "expert", split_axis=0, concat_axis=0, tiled=True)
    slot_rows = arrived.transpose(1, 0, 2, 3).reshape(
        local_experts, owners * lane_rows, model_width
    )
    all_rows = lax.all_gather(slot_rows, "ctx", axis=1, tiled=True)
    gate_pre = jnp.einsum("erd,edf->erf", all_rows, gate_weight, preferred_element_type=jnp.float32)
    up_pre = jnp.einsum("erd,edf->erf", all_rows, up_weight, preferred_element_type=jnp.float32)
    hidden_float, act_back = jax.vjp(gated_hidden, gate_pre, up_pre)
    hidden_act = hidden_float.astype(jnp.bfloat16)
    partial_value = jnp.einsum(
        "erf,efd->erd", hidden_act, down_weight, preferred_element_type=jnp.float32
    )
    expert_result = lax.psum_scatter(partial_value, "ctx", scatter_dimension=1, tiled=True).astype(
        jnp.bfloat16
    )
    returning = expert_result.reshape(local_experts, owners, lane_rows, model_width).transpose(
        1, 0, 2, 3
    )
    upstream = cotangent.astype(jnp.float32).reshape(tok_count, model_width)
    scaled_grad = (
        (gate_values[:, :, None] * upstream[:, None, :])
        .reshape(tok_count * 2, model_width)
        .astype(jnp.bfloat16)
    )
    padded_grad = jnp.concatenate([scaled_grad, jnp.zeros((1, model_width), jnp.bfloat16)], axis=0)
    grad_slots = jnp.take(padded_grad, slot_source, axis=0).reshape(
        owners, local_experts, lane_rows, model_width
    )
    returned, grad_arrived = (
        lax.all_to_all(returning, "expert", split_axis=0, concat_axis=0, tiled=True),
        lax.all_to_all(grad_slots, "expert", split_axis=0, concat_axis=0, tiled=True),
    )
    picked = (
        jnp.take(returned.reshape(buffer_rows, model_width), target_flat, axis=0)
        .reshape(tok_count, 2, model_width)
        .astype(jnp.float32)
    )
    expert_sum = jnp.sum(gate_values[:, :, None] * picked, axis=1)
    layer_output = (hidden_state + expert_sum.reshape(seq_count, pos_count, model_width)).astype(
        jnp.bfloat16
    )
    pair_delta = jnp.sum(upstream[:, None, :] * picked, axis=-1)
    (pick_grad,) = gate_back(pair_delta)
    expert_iota = lax.iota(jnp.int32, expert_num)[None, None, :]
    logit_grad = jnp.sum(
        jnp.where(routed_ids[:, :, None] == expert_iota, pick_grad[:, :, None], 0.0), axis=1
    ).astype(jnp.bfloat16)
    router_part = jnp.einsum(
        "td,te->de", expert_input, logit_grad, preferred_element_type=jnp.float32
    )
    expert_delta = jnp.einsum(
        "te,de->td", logit_grad, router_weight, preferred_element_type=jnp.float32
    )
    slot_grads = grad_arrived.transpose(1, 0, 2, 3).reshape(
        local_experts, owners * lane_rows, model_width
    )
    all_grads = lax.all_gather(slot_grads, "ctx", axis=1, tiled=True)
    hidden_grad = jnp.einsum(
        "erd,efd->erf", all_grads, down_weight, preferred_element_type=jnp.float32
    )
    gate_delta, up_delta = act_back(hidden_grad)
    gate_low = gate_delta.astype(jnp.bfloat16)
    up_low = up_delta.astype(jnp.bfloat16)
    down_part = jnp.einsum(
        "erf,erd->efd", hidden_act, all_grads, preferred_element_type=jnp.float32
    )
    gate_part = jnp.einsum("erd,erf->edf", all_rows, gate_low, preferred_element_type=jnp.float32)
    up_part = jnp.einsum("erd,erf->edf", all_rows, up_low, preferred_element_type=jnp.float32)
    row_part = jnp.einsum(
        "erf,edf->erd", gate_low, gate_weight, preferred_element_type=jnp.float32
    ) + jnp.einsum("erf,edf->erd", up_low, up_weight, preferred_element_type=jnp.float32)
    row_grads = lax.psum_scatter(row_part, "ctx", scatter_dimension=1, tiled=True).astype(
        jnp.bfloat16
    )
    gate_grad, up_grad, down_grad = (
        lax.psum_scatter(
            gate_part.astype(jnp.bfloat16), "dp", scatter_dimension=1, tiled=True
        ).astype(jnp.float32),
        lax.psum_scatter(
            up_part.astype(jnp.bfloat16), "dp", scatter_dimension=1, tiled=True
        ).astype(jnp.float32),
        lax.psum_scatter(
            down_part.astype(jnp.bfloat16), "dp", scatter_dimension=2, tiled=True
        ).astype(jnp.float32),
    )
    back_rows = row_grads.reshape(local_experts, owners, lane_rows, model_width).transpose(
        1, 0, 2, 3
    )
    returned_grads = lax.all_to_all(back_rows, "expert", split_axis=0, concat_axis=0, tiled=True)
    token_grads = (
        jnp.take(returned_grads.reshape(buffer_rows, model_width), target_flat, axis=0)
        .reshape(tok_count, 2, model_width)
        .astype(jnp.float32)
    )
    expert_delta = expert_delta + jnp.sum(token_grads, axis=1)
    state_part, second_part = second_back(expert_delta.reshape(seq_count, pos_count, model_width))
    state_grad = state_part + upstream.reshape(seq_count, pos_count, model_width)
    state_low = state_grad.astype(jnp.bfloat16)
    merge_part = jnp.einsum(
        "spd,spe->de", mixed_heads, state_low, preferred_element_type=jnp.float32
    )
    mixed_flat = jnp.einsum(
        "spe,de->spd", state_low, merge_weight, preferred_element_type=jnp.float32
    ).astype(jnp.bfloat16)
    mixed_grad = mixed_flat.reshape(seq_count, pos_count, heads_num, head_dimension)
    masked_again = score_grid()
    prob_again = jnp.exp(masked_again - log_total)
    prob_grad = jnp.einsum(
        "sqhd,skhd->shqk", mixed_grad, value_heads, preferred_element_type=jnp.float32
    )
    row_dot = jnp.sum(prob_again * prob_grad, axis=-1, keepdims=True)
    score_grad = (prob_again * (prob_grad - row_dot)).astype(jnp.bfloat16)
    query_back = (
        (
            jnp.einsum("shqk,skhd->sqhd", score_grad, key_heads, preferred_element_type=jnp.float32)
            * score_scale
        )
        .astype(jnp.bfloat16)
        .reshape(seq_count, pos_count, model_width)
    )
    bias_accumulated = jnp.sum(score_grad.astype(jnp.float32), axis=0)
    bias_portion = jnp.einsum(
        "tey,aey->at", bias_accumulated, bucket_onehot, precision=highest_precision
    )
    total_rows = log_total[..., 0].transpose(0, 2, 1)
    dot_rows = row_dot[..., 0].transpose(0, 2, 1)
    total_whole, dot_whole = (
        lax.all_gather(total_rows, ("ctx", "dp"), axis=1, tiled=True),
        lax.all_gather(dot_rows, ("ctx", "dp"), axis=1, tiled=True),
    )
    own_keys = keys_local.reshape(seq_count, pos_count, heads_num, head_dimension)
    own_values = values_local.reshape(seq_count, pos_count, heads_num, head_dimension)
    own_pos = first_pos + lax.iota(jnp.int32, pos_count)
    empty = jnp.zeros((seq_count, pos_count, heads_num, head_dimension), jnp.float32)
    key_acc = empty
    value_acc = empty
    query_piece = lax.all_gather(queries, ("ctx", "dp"), axis=1, tiled=True)
    grad_piece = lax.all_gather(mixed_flat, ("ctx", "dp"), axis=1, tiled=True)
    row_count = query_piece.shape[1]
    query_part_heads = query_piece.reshape(seq_count, row_count, heads_num, head_dimension)
    grad_part_heads = grad_piece.reshape(seq_count, row_count, heads_num, head_dimension)
    total_piece = lax.slice_in_dim(total_whole, 0, row_count, axis=1).transpose(0, 2, 1)[..., None]
    dot_piece = lax.slice_in_dim(dot_whole, 0, row_count, axis=1).transpose(0, 2, 1)[..., None]
    piece_pos = lax.iota(jnp.int32, row_count)
    gap = piece_pos[:, None] - own_pos[None, :]
    seen = gap >= 0
    piece_hot = bucket_table(jnp.clip(gap, 0, seq_len - 1), bucket_num)
    piece_bias = jnp.einsum(
        "ry,rta->yta", relative_bucket_bias, piece_hot, precision=highest_precision
    )
    raw_scores = (
        jnp.einsum(
            "sqhd,skhd->shqk", query_part_heads, own_keys, preferred_element_type=jnp.float32
        )
        * score_scale
        + piece_bias[None]
    )
    masked_piece = jnp.where(seen[None, None], raw_scores, -1e30)
    prob_piece = jnp.exp(masked_piece - total_piece)
    grad_prob = jnp.einsum(
        "sqhd,skhd->shqk", grad_part_heads, own_values, preferred_element_type=jnp.float32
    )
    score_piece = (prob_piece * (grad_prob - dot_piece)).astype(jnp.bfloat16)
    key_acc = (
        key_acc
        + jnp.einsum(
            "shqk,sqhd->skhd", score_piece, query_part_heads, preferred_element_type=jnp.float32
        )
        * score_scale
    )
    value_acc = value_acc + jnp.einsum(
        "shqk,sqhd->skhd",
        prob_piece.astype(jnp.bfloat16),
        grad_part_heads,
        preferred_element_type=jnp.float32,
    )
    key_back = key_acc.reshape(seq_count, pos_count, model_width).astype(jnp.bfloat16)
    value_back = value_acc.reshape(seq_count, pos_count, model_width).astype(jnp.bfloat16)
    query_part = jnp.einsum("spd,spe->de", mixer_in, query_back, preferred_element_type=jnp.float32)
    key_part = jnp.einsum("spd,spe->de", mixer_in, key_back, preferred_element_type=jnp.float32)
    value_part = jnp.einsum("spd,spe->de", mixer_in, value_back, preferred_element_type=jnp.float32)
    mixer_delta = jnp.einsum(
        "spe,de->spd", query_back, query_weight, preferred_element_type=jnp.float32
    )
    mixer_delta = mixer_delta + jnp.einsum(
        "spe,de->spd", key_back, key_weight, preferred_element_type=jnp.float32
    )
    mixer_delta = mixer_delta + jnp.einsum(
        "spe,de->spd", value_back, value_weight, preferred_element_type=jnp.float32
    )
    input_part, first_part = first_back(mixer_delta)
    input_grad = state_grad + input_part
    stacked = jnp.stack([query_part, key_part, value_part, merge_part])
    blocked = (
        stacked.reshape(4, places, model_width // places, owners, model_width // owners)
        .transpose(3, 1, 0, 2, 4)
        .reshape(owners * places, 4, model_width // places, model_width // owners)
    )
    dense_sums = lax.psum_scatter(
        blocked, ("expert", "ctx", "dp"), scatter_dimension=0, tiled=True
    )[0]
    first_sum, second_sum, router_sum, bias_total = lax.psum(
        (first_part, second_part, router_part, bias_portion), ("expert", "ctx", "dp")
    )
    return (
        layer_output,
        input_grad,
        first_sum,
        dense_sums[0],
        dense_sums[1],
        dense_sums[2],
        dense_sums[3],
        bias_total,
        second_sum,
        router_sum,
        gate_grad,
        up_grad,
        down_grad,
    )


def solution(mesh):
    in_specs = (
        P("expert", ("ctx", "dp"), None),
        P("expert", ("ctx", "dp"), None),
        P("expert", ("ctx", "dp"), None),
        P(),
        P(),
        P(),
        P(),
        P(),
        P(),
        P(),
        P(),
        P("expert", None, "ctx"),
        P("expert", None, "ctx"),
        P("expert", "ctx", None),
    )
    out_specs = (
        P("expert", ("ctx", "dp"), None),
        P("expert", ("ctx", "dp"), None),
        P(),
        P(("ctx", "dp"), "expert"),
        P(("ctx", "dp"), "expert"),
        P(("ctx", "dp"), "expert"),
        P(("ctx", "dp"), "expert"),
        P(),
        P(),
        P(),
        P("expert", "dp", "ctx"),
        P("expert", "dp", "ctx"),
        P("expert", "ctx", "dp"),
    )
    return jax.shard_map(
        per_device, mesh=mesh, in_specs=in_specs, out_specs=out_specs, check_vma=False
    )
```

profile of v0, /device:TPU:0, one launch (start us, length us, event | category | flops | bytes accessed | tf_op | source)
XLA Modules:
  0.0 560.5 jit_solution(13332193181883512422)
XLA Ops:
  21.3 7.8 %fusion.1 = f32[128,1024,12]{1,2,0:T(8,128)} fusion(s32[128,1024]{1,0:T(8,128)S(1)} %convert_add_fusion.1, f32[32,12]{0,1:T(8,128)S(1)} %copy-done.28), kind=kOutput, calls=%fused_computation.8 | convolution fusion | flops 608174080 | bytes 6817280 | tf_op jit(solution)/shard_map/ry,rta->yta/dot_general | solution.py:108
  29.2 10.4 %all-gather.17.cloned.1.call-done = bf16[1024,768]{1,0:T(8,128)(2,1)} async-done(((bf16[128,768]{1,0:T(8,128)(2,1)}), bf16[1024,768]{1,0:T(8,128)(2,1)}) %all-gather.17.cloned.1.call-update) | async-done | bytes 1572880 | tf_op jit(solution)/shard_map/all_gather | solution.py:96
  41.6 8.7 %fusion.181 = (f32[12,128]{1,0:T(8,128)S(1)}, f32[12,128,1024]{2,1,0:T(8,128)S(1)}) fusion(f32[128,1024,12]{1,2,0:T(8,128)} %fusion.1, bf16[128,12,64]{0,2,1:T(8,128)(2,1)S(1)} %bitcast.326, bf16[1024,12,64]{0,2,1:T(8,128)(2,1)S(1)} %bitcast.304, pred[128,1024]{1,0:T(8,128)(4,1)S(1)} %fusion.108), kind=kOutput, calls=%fused_computation.282 | convolution fusion | flops 207616512 | bytes 14489600 | tf_op jit(solution)/shard_map/sqhd,skhd->shqk/dot_general | solution.py:114
  54.4 13.3 %all-gather.15.cloned.1.call-done = bf16[1024,768]{1,0:T(8,128)(2,1)} async-done(((bf16[128,768]{1,0:T(8,128)(2,1)}), bf16[1024,768]{1,0:T(8,128)(2,1)}) %all-gather.15.cloned.1.call-update) | async-done | bytes 1572880 | tf_op jit(solution)/shard_map/all_gather | solution.py:97
  77.9 17.7 %all_to_all.20 = bf16[4,1,72,768]{3,2,1,0:T(8,128)(2,1)} all-to-all(bf16[4,1,72,768]{3,2,1,0:T(8,128)(2,1)S(1)} %broadcast_select_fusion.1), channel_id=1, replica_groups=mesh['expert'=4,'ctx'=4,'dp'=2] {'expert'}, dimensions={0} | all-to-all | bytes 884736 | tf_op jit(solution)/shard_map/all_to_all | solution.py:165
  106.0 15.4 %all_to_all.21 = bf16[4,1,72,768]{3,2,1,0:T(8,128)(2,1)} all-to-all(bf16[4,1,72,768]{3,2,1,0:T(8,128)(2,1)S(1)} %broadcast_select_fusion), channel_id=1, replica_groups=mesh['expert'=4,'ctx'=4,'dp'=2] {'expert'}, dimensions={0} | all-to-all | bytes 884736 | tf_op jit(solution)/shard_map/all_to_all | solution.py:195
  122.0 5.1 fusion.36
  127.1 13.4 %all-gather.13.cloned.1.call-done = bf16[1,1152,768]{2,1,0:T(8,128)(2,1)} async-done(((bf16[1,288,768]{2,1,0:T(8,128)(2,1)}), bf16[1,1152,768]{2,1,0:T(8,128)(2,1)}) %all-gather.13.cloned.1.call-update) | async-done | bytes 1769488 | tf_op jit(solution)/shard_map/all_gather | solution.py:221
  140.5 10.1 %multiply_convert_fusion.2 = (bf16[1152,768]{1,0:T(8,128)(2,1)S(1)}, f32[1152,768]{1,0:T(8,128)S(1)}, f32[1152,768]{1,0:T(8,128)S(1)}) fusion(f32[1152,768]{1,0:T(8,128)} %fusion.36, bf16[1,768,768]{2,1,0:T(8,128)(2,1)S(1)} %copy-done, bf16[1,1152,768]{2,1,0:T(8,128)(2,1)} %all-gather.13.cloned.1.call-done), kind=kOutput, calls=%fused_computation.33 | convolution fusion | flops 1417347072 | bytes 15335424 | tf_op jit(solution)/shard_map/erd,efd->erf/dot_general | solution.py:222
  164.6 35.7 %reduce-scatter.11.cloned.1.call-done = f32[1,288,768]{2,1,0:T(8,128)} async-done(((f32[1,1152,768]{2,1,0:T(8,128)}), f32[1,288,768]{2,1,0:T(8,128)}) %reduce-scatter.11.cloned.1.call-update) | async-done | bytes 884752 | tf_op jit(solution)/shard_map/reduce_scatter | solution.py:236
  206.8 36.5 %reduce-scatter.9.cloned.1.call-done = f32[1,288,768]{2,1,0:T(8,128)} async-done(((f32[1,1152,768]{2,1,0:T(8,128)}), f32[1,288,768]{2,1,0:T(8,128)}) %reduce-scatter.9.cloned.1.call-update) | async-done | bytes 884752 | tf_op jit(solution)/shard_map/reduce_scatter | solution.py:177
  252.8 9.8 %all-to-all-done.1 = bf16[4,1,72,768]{3,2,1,0:T(8,128)(2,1)S(1)} async-done(((bf16[4,1,72,768]{3,2,1,0:T(8,128)(2,1)}), bf16[4,1,72,768]{3,2,1,0:T(8,128)(2,1)S(1)}, u32[]{:S(2)}, u32[]{:S(2)}) %all-to-all-start.1) | async-done | bytes 442400 | tf_op jit(solution)/shard_map/all_to_all | solution.py:194
  292.5 4.9 fusion.53
  300.5 7.3 %fusion.2 = f32[1024,128,12]{1,2,0:T(8,128)} fusion(s32[1024,128]{1,0:T(8,128)S(1)} %convert_add_fusion, f32[32,12]{0,1:T(8,128)S(1)} %copy-done.29), kind=kOutput, calls=%fused_computation.9 | convolution fusion | flops 608174080 | bytes 6817280 | tf_op jit(solution)/shard_map/ry,rta->yta/dot_general | solution.py:312
  309.5 13.0 %all_gather.29 = f32[1,1024,12]{1,2,0:T(8,128)S(1)} all-gather(f32[1,128,12]{1,2,0:T(8,128)S(1)} %bitcast.335), channel_id=1, replica_groups=mesh['expert'=4,'ctx'=4,'dp'=2] {'ctx','dp'}, dimensions={1}, use_global_device_ids=true | all-gather | bytes 55296 | tf_op jit(solution)/shard_map/all_gather | solution.py:292
  322.5 9.1 %fusion.8 = f32[12,1024,128]{2,1,0:T(8,128)} fusion(f32[1024,128,12]{1,2,0:T(8,128)} %fusion.2, f32[12,1024]{1,0:T(8,128)S(1)} %bitcast.334, pred[1024,128]{1,0:T(8,128)(4,1)S(1)} %fusion.75, bf16[1024,12,64]{0,2,1:T(8,128)(2,1)S(1)} %bitcast.302, bf16[128,12,64]{0,2,1:T(8,128)(2,1)S(1)} %bitcast.327), kind=kOutput, calls=%fused_computation.17 | convolution fusion | flops 207618048 | bytes 14532608 | tf_op jit(solution)/shard_map/sqhd,skhd->shqk/dot_general | solution.py:316
  334.6 5.2 multiply_reduce_fusion
  344.8 15.9 %all_gather.31 = f32[1,1024,12]{1,2,0:T(8,128)} all-gather(f32[1,128,12]{1,2,0:T(8,128)S(1)} %bitcast.336), channel_id=1, replica_groups=mesh['expert'=4,'ctx'=4,'dp'=2] {'ctx','dp'}, dimensions={1}, use_global_device_ids=true | all-gather | bytes 55296 | tf_op jit(solution)/shard_map/all_gather | solution.py:293
  366.7 6.3 %fusion.65 = bf16[12,64,128]{2,1,0:T(8,128)(2,1)S(1)} fusion(bf16[1024,12,64]{0,2,1:T(8,128)(2,1)S(1)} %bitcast.303, f32[12,1024,128]{2,1,0:T(8,128)} %fusion.8, f32[12,1024]{1,0:T(8,128)} %bitcast.333, bf16[1024,12,64]{0,2,1:T(8,128)(2,1)} %bitcast.306, bf16[128,12,64]{0,2,1:T(8,128)(2,1)} %bitcast.332), kind=kOutput, calls=%fused_computation.94 | convolution fusion | flops 407568384 | bytes 9879552 | tf_op jit(solution)/shard_map/shqk,sqhd->skhd/dot_general | solution.py:330
  381.9 4.8 maximum_bitcast_fusion
  386.7 10.7 %copy.142 = f32[4,8,4,96,192]{4,3,2,1,0:T(8,128)} copy(f32[4,8,4,96,192]{4,3,0,1,2:T(8,128)} %maximum_bitcast_fusion) | data formatting | bytes 18874368 | tf_op jit(solution)/shard_map/transpose | solution.py:360
  409.1 6.8 %fusion.71 = f32[32,12]{0,1:T(8,128)S(1)} fusion(bf16[12,128,1024]{2,1,0:T(8,128)(2,1)} %copy-done.6, s32[128,1024]{1,0:T(8,128)S(1)} %copy-done.16), kind=kOutput, calls=%fused_computation.102 | convolution fusion | flops 104857600 | bytes 3671552 | tf_op jit(solution)/shard_map/tey,aey->at/dot_general | solution.py:286
  415.9 37.8 %all-reduce.2 = (f32[768]{0:T(1024)}, f32[32,12]{0,1:T(8,128)}, f32[768]{0:T(1024)}, f32[768,4]{0,1:T(4,128)}) all-reduce(f32[768]{0:T(1024)S(1)} %get-tuple-element.16, f32[32,12]{0,1:T(8,128)S(1)} %fusion.71, f32[768]{0:T(1024)S(1)} %copy-done.35, ...), channel_id=1, replica_groups=mesh['expert'=4,'ctx'=4,'dp'=2] {'expert','ctx','dp'}, use_global_device_ids=true, to_apply=%region_22.24 | all-reduce | flops 4992 | bytes 39936 | tf_op jit(solution)/shard_map/psum | solution.py:366
  454.7 97.1 %reduce-scatter.13.cloned.1.call-done = f32[1,4,96,192]{3,2,1,0:T(8,128)} async-done(((f32[32,4,96,192]{3,2,1,0:T(8,128)}), f32[1,4,96,192]{3,2,1,0:T(8,128)}) %reduce-scatter.13.cloned.1.call-update) | async-done | bytes 294928 | tf_op jit(solution)/shard_map/reduce_scatter | solution.py:363
  (286 shorter events, 142.3 us)
Async XLA Ops:
  7.2 133.3 %copy-start = (bf16[1,768,768]{2,1,0:T(8,128)(2,1)S(1)}, bf16[1,768,768]{2,1,0:T(8,128)(2,1)}, u32[]{:S(2)}) copy-start(bf16[1,768,768]{2,1,0:T(8,128)(2,1)} %param.29) | copy-start | bytes 3538948
  7.3 32.3 %all-gather.17.cloned.1.call-start = ((), (), s32[]{:S(2)}) async-start(), calls=%async_computation.18 | async-start | bytes 1769472 | tf_op jit(solution)/shard_map/all_gather | solution.py:96
  11.0 56.7 %all-gather.15.cloned.1.call-start = ((), (), s32[]{:S(2)}) async-start(), calls=%async_computation.17 | async-start | bytes 1769472 | tf_op jit(solution)/shard_map/all_gather | solution.py:97
  13.5 108.5 %all-gather.11.cloned.1.call-start = ((), (), s32[]{:S(2)}) async-start(), calls=%async_computation.10 | async-start | bytes 2211840 | tf_op jit(solution)/shard_map/all_gather | solution.py:169
  75.3 20.2 %copy-start.48 = (f32[128]{0:T(128)}, f32[128]{0:T(128)S(1)}, u32[]{:S(2)}) copy-start(f32[128]{0:T(128)S(1)} %fusion.173) | copy-start | bytes 1540
  75.3 20.3 %copy-start.25 = (bf16[1,128,768]{2,1,0:T(8,128)(2,1)S(1)}, bf16[1,128,768]{2,1,0:T(8,128)(2,1)}, u32[]{:S(2)}) copy-start(bf16[1,128,768]{2,1,0:T(8,128)(2,1)} %param.17) | copy-start | bytes 589828
  77.7 20.8 %copy-start.37 = (s32[1,128,2]{1,2,0:T(2,128)S(1)}, s32[1,128,2]{1,2,0:T(2,128)}, u32[]{:S(2)}) copy-start(s32[1,128,2]{1,2,0:T(2,128)} %param.18) | copy-start | bytes 3076
  77.7 21.1 %copy-start.34 = (bf16[768,4]{0,1:T(4,128)(2,1)S(1)}, bf16[768,4]{0,1:T(4,128)(2,1)}, u32[]{:S(2)}) copy-start(bf16[768,4]{0,1:T(4,128)(2,1)} %param.26) | copy-start | bytes 18436
  95.6 44.9 %all-gather.13.cloned.1.call-start = ((), (), s32[]{:S(2)}) async-start(), calls=%async_computation.12 | async-start | bytes 2211840 | tf_op jit(solution)/shard_map/all_gather | solution.py:221
  121.4 78.8 %reduce-scatter.11.cloned.1.call-start = ((), (), s32[]{:S(2)}) async-start(), calls=%async_computation.13 | async-start | bytes 4423680 | tf_op jit(solution)/shard_map/reduce_scatter | solution.py:236
  159.6 83.6 %reduce-scatter.9.cloned.1.call-start = ((), (), s32[]{:S(2)}) async-start(), calls=%async_computation.11 | async-start | bytes 4423680 | tf_op jit(solution)/shard_map/reduce_scatter | solution.py:177
  164.5 86.3 %copy-start.44 = (s32[256]{0:T(256)S(1)}, s32[256]{0:T(256)}, u32[]{:S(2)}) copy-start(s32[256]{0:T(256)} %copy-done.43) | copy-start | bytes 3076
  202.2 43.1 %all-to-all-start.3 = ((bf16[4,1,72,768]{3,2,1,0:T(8,128)(2,1)}), bf16[4,1,72,768]{3,2,1,0:T(8,128)(2,1)S(1)}, u32[]{:S(2)}, u32[]{:S(2)}) async-start(bf16[4,1,72,768]{3,2,1,0:T(8,128)(2,1)} %bitcast.36), calls=%async_computation.5 | async-start | bytes 884736 | tf_op jit(solution)/shard_map/all_to_all | solution.py:253
  245.2 17.3 %all-to-all-start.1 = ((bf16[4,1,72,768]{3,2,1,0:T(8,128)(2,1)}), bf16[4,1,72,768]{3,2,1,0:T(8,128)(2,1)S(1)}, u32[]{:S(2)}, u32[]{:S(2)}) async-start(bf16[4,1,72,768]{3,2,1,0:T(8,128)(2,1)} %bitcast.321), calls=%async_computation.2 | async-start | bytes 884736 | tf_op jit(solution)/shard_map/all_to_all | solution.py:194
  249.8 57.9 %all-gather.19.cloned.1.call-start = ((), (), s32[]{:S(2)}) async-start(), calls=%async_computation.19 | async-start | bytes 1769472 | tf_op jit(solution)/shard_map/all_gather | solution.py:301
  250.6 113.5 %all-gather.21.cloned.1.call-start = ((), (), s32[]{:S(2)}) async-start(), calls=%async_computation.20 | async-start | bytes 1769472 | tf_op jit(solution)/shard_map/all_gather | solution.py:302
  281.1 116.4 %reduce-scatter.19.cloned.1.call-start = ((), (), s32[]{:S(2)}) async-start(), calls=%async_computation.21 | async-start | bytes 1769472
  292.4 112.1 %reduce-scatter.15.cloned.1.call-start = ((), (), s32[]{:S(2)}) async-start(), calls=%async_computation.15 | async-start | bytes 1769472 | tf_op jit(solution)/shard_map/reduce_scatter | solution.py:240
  297.4 109.4 %reduce-scatter.17.cloned.1.call-start = ((), (), s32[]{:S(2)}) async-start(), calls=%async_computation.16 | async-start | bytes 1769472 | tf_op jit(solution)/shard_map/reduce_scatter | solution.py:243
  334.4 217.3 %reduce-scatter.13.cloned.1.call-start = ((), (), s32[]{:S(2)}) async-start(), calls=%async_computation.14 | async-start | bytes 12976128 | tf_op jit(solution)/shard_map/reduce_scatter | solution.py:363
  341.4 20.4 %copy-start.24 = (bf16[12,64,128]{2,1,0:T(8,128)(2,1)S(1)}, bf16[12,64,128]{2,1,0:T(8,128)(2,1)}, u32[]{:S(2)}) copy-start(bf16[12,64,128]{2,1,0:T(8,128)(2,1)} %copy-done.23) | copy-start | bytes 589828
  409.1 44.7 %copy-start.52 = (f32[128]{0:T(128)S(1)}, f32[128]{0:T(128)}, u32[]{:S(2)}) copy-start(f32[128]{0:T(128)} %copy-done.51) | copy-start | bytes 1540
  409.1 44.7 %copy-start.18 = (f32[1,128,768]{2,1,0:T(8,128)S(1)}, f32[1,128,768]{2,1,0:T(8,128)}, u32[]{:S(2)}) copy-start(f32[1,128,768]{2,1,0:T(8,128)} %copy-done.17) | copy-start | bytes 1179652
  409.1 144.4 %copy-start.1 = (bf16[1,768,768]{2,1,0:T(8,128)(2,1)S(1)}, bf16[1,768,768]{2,1,0:T(8,128)(2,1)}, u32[]{:S(2)}) copy-start(bf16[1,768,768]{2,1,0:T(8,128)(2,1)} %param.29) | copy-start | bytes 3538948
  (54 other events, 348.2 us)
Sparse Core Ops, SparseCore 0:
  11.1 28.3 all-gather.16
  42.0 25.6 all-gather.14
  95.7 18.9 all-gather.10
  121.6 18.8 all-gather.12
  159.8 40.4 reduce-scatter.10
  202.8 40.4 reduce-scatter.8
  252.6 26.1 all-gather.18
  281.2 25.1 all-gather.20
  309.2 21.7 reduce-scatter.18
  333.8 21.9 reduce-scatter.14
  358.0 21.7 reduce-scatter.16
  397.6 154.0 reduce-scatter.12
where the time goes:
time: 568 us; the launch traced here: 561 us
  waiting for transfers between devices  217 us (38%)
  matrix products  118 us (21%)
  blocking collectives  99.8 us (18%)
  local copies, waits for them, and re-layouts  61.3 us (11%)
  other arithmetic  38.6 us (7%)
  between operations  15.5 us (3%)
  starting transfers between devices  10.6 us (2%)
    reduce_scatter x1, waiting for transfers between devices, per_device(): lax.psum_scatter(blocked, ('expert', 'ctx', 'dp'), scatter_dimension=0, t...  97.1 us
    psum x1, blocking collectives, per_device(): lax.psum((first_part, second_part, router_part, bias_portion), ('expert',...  37.8 us
    reduce_scatter x1, waiting for transfers between devices, per_device(): lax.psum_scatter(partial_value, 'ctx', scatter_dimension=1, tiled=True)  36.5 us
    reduce_scatter x1, waiting for transfers between devices, per_device(): lax.psum_scatter(row_part, 'ctx', scatter_dimension=1, tiled=True)  35.7 us
    unnamed x133, local copies, waits for them, and re-layouts  19.5 us
    all_to_all x1, blocking collectives, per_device(): lax.all_to_all(dispatched, 'expert', split_axis=0, concat_axis=0, tiled=T...  17.7 us
    all_gather x1, blocking collectives, per_device(): lax.all_gather(dot_rows, ('ctx', 'dp'), axis=1, tiled=True)  15.9 us
    all_to_all x1, blocking collectives, per_device(): lax.all_to_all(grad_slots, 'expert', split_axis=0, concat_axis=0, tiled=T...  15.4 us
  transfers between devices with their start and end apart: 14, of which 7 were waited for; matrix products, arithmetic and copies ran while one was open for 32% of the time, Pallas kernels for 0%

commit v1 on v0

v1 whole, which is shorter than its diff:
```python
import math

import jax
import jax.numpy as jnp
from jax import lax
from jax.sharding import PartitionSpec as P

norm_eps = 1e-06
reach_span = 128.0


def bucket_bounds(bucket_num):
    exact_span = bucket_num // 2
    bounds = list(range(1, exact_span))
    for target in range(exact_span, bucket_num):
        border = exact_span
        while (
            exact_span
            + int(math.log(border / exact_span) / math.log(reach_span / exact_span) * exact_span)
            < target
        ):
            border += 1
        bounds.append(border)
    return bounds


def distance_buckets(distance, bucket_num):
    counted = jnp.zeros(distance.shape, jnp.int32)
    for border in bucket_bounds(bucket_num):
        counted = counted + (distance >= border).astype(jnp.int32)
    return counted


def rms_scale(values, gain_vec):
    return (
        values * lax.rsqrt(jnp.mean(values * values, axis=-1, keepdims=True) + norm_eps) * gain_vec
    )


def gated_hidden(gate_pre, up_pre):
    return jax.nn.gelu(gate_pre, approximate=False) * up_pre


def pair_softmax(logit_pair):
    return jax.nn.softmax(logit_pair, axis=-1)


def bucket_table(distance, bucket_num):
    bucket_of = distance_buckets(distance, bucket_num)
    return (lax.iota(jnp.int32, bucket_num)[:, None, None] == bucket_of[None]).astype(jnp.float32)


def split_parts(values, count):
    parts = []
    rest = values
    for _ in range(count):
        part = rest.astype(jnp.bfloat16)
        parts.append(part)
        rest = rest - part.astype(jnp.float32)
    return parts


def bias_grid(bias_table, distance):
    bucket_num = bias_table.shape[0]
    hot = bucket_table(distance, bucket_num).astype(jnp.bfloat16)
    table = jnp.concatenate(split_parts(bias_table, 3), axis=0)
    return jnp.einsum(
        "ry,rta->yta",
        table,
        jnp.concatenate([hot, hot, hot], axis=0),
        preferred_element_type=jnp.float32,
    )


def slot_hot(hits, capacity):
    pos_count = hits.shape[-1]
    before = (
        lax.iota(jnp.int32, pos_count)[:, None] < lax.iota(jnp.int32, pos_count)[None, :]
    ).astype(jnp.bfloat16)
    slots = jnp.einsum(
        "...p,pq->...q", hits.astype(jnp.bfloat16), before, preferred_element_type=jnp.float32
    ).astype(jnp.int32)
    rows = lax.iota(jnp.int32, capacity)[:, None]
    return jnp.where(
        hits[..., None, :] & (slots[..., None, :] == rows), 1.0, 0.0
    ).astype(jnp.bfloat16)


def total_over(values, axes):
    flat = jnp.concatenate([value.reshape(-1) for value in values])
    size = flat.shape[0]
    pad = (-size) % 1024
    packed = jnp.pad(flat, (0, pad)).reshape(1, -1, 128)
    summed = jnp.sum(lax.all_gather(packed, axes, axis=0, tiled=True), axis=0).reshape(-1)
    outs = []
    offset = 0
    for value in values:
        outs.append(summed[offset : offset + value.size].reshape(value.shape))
        offset += value.size
    return outs


def per_device(
    inputs,
    cotangent,
    expert_ids,
    first_gain,
    query_weight,
    key_weight,
    value_weight,
    merge_weight,
    relative_bucket_bias,
    expert_norm_gain,
    router_weight,
    gate_weight,
    up_weight,
    down_weight,
):
    seq_count, pos_count, model_width = inputs.shape
    bucket_num, heads_num = relative_bucket_bias.shape
    head_dimension = model_width // heads_num
    score_scale = head_dimension ** (-0.5)
    expert_num = router_weight.shape[1]
    local_experts = gate_weight.shape[0]
    owners = lax.axis_size("expert")
    places = lax.axis_size(("ctx", "dp"))
    seq_len = pos_count * places
    capacity = min(pos_count, max(2, 9 * pos_count // (4 * expert_num)))
    lane_rows = seq_count * capacity
    everyone = ("expert", "ctx", "dp")
    column_count = model_width // owners
    first_expert = lax.axis_index("expert") * local_experts
    ids_all = lax.all_gather(expert_ids, ("ctx", "expert"), axis=0, tiled=True)
    block_num = ids_all.shape[0]
    residual = inputs.astype(jnp.float32)
    first_normed, first_back = jax.vjp(rms_scale, residual, first_gain)
    mixer_in = first_normed.astype(jnp.bfloat16)
    keys_local = jnp.einsum(
        "spd,de->spe", mixer_in, key_weight, preferred_element_type=jnp.float32
    ).astype(jnp.bfloat16)
    values_local = jnp.einsum(
        "spd,de->spe", mixer_in, value_weight, preferred_element_type=jnp.float32
    ).astype(jnp.bfloat16)
    keys_whole, values_whole = (
        lax.all_gather(keys_local, ("ctx", "dp"), axis=1, tiled=True),
        lax.all_gather(values_local, ("ctx", "dp"), axis=1, tiled=True),
    )
    queries = jnp.einsum(
        "spd,de->spe", mixer_in, query_weight, preferred_element_type=jnp.float32
    ).astype(jnp.bfloat16)
    query_heads = queries.reshape(seq_count, pos_count, heads_num, head_dimension)
    key_heads = keys_whole.reshape(seq_count, seq_len, heads_num, head_dimension)
    value_heads = values_whole.reshape(seq_count, seq_len, heads_num, head_dimension)
    first_pos = lax.axis_index(("ctx", "dp")) * pos_count
    query_pos = first_pos + lax.iota(jnp.int32, pos_count)
    offsets = query_pos[:, None] - lax.iota(jnp.int32, seq_len)[None, :]
    visible = offsets >= 0
    distance = jnp.clip(offsets, 0, seq_len - 1)
    bias_lattice = bias_grid(relative_bucket_bias, distance)
    raw_scores = (
        jnp.einsum("sqhd,skhd->shqk", query_heads, key_heads, preferred_element_type=jnp.float32)
        * score_scale
        + bias_lattice[None]
    )
    masked = jnp.where(visible[None, None], raw_scores, -1e30)
    row_top = jnp.max(masked, axis=-1, keepdims=True)
    exp_terms = jnp.exp(masked - row_top)
    row_total = jnp.sum(exp_terms, axis=-1, keepdims=True)
    prob_mass = exp_terms / row_total
    log_total = row_top + jnp.log(row_total)
    attended = jnp.einsum(
        "shqk,skhd->sqhd",
        prob_mass.astype(jnp.bfloat16),
        value_heads,
        preferred_element_type=jnp.float32,
    )
    total_rows = log_total[..., 0].transpose(0, 2, 1)
    stat_pad = -(-3 * heads_num // 128) * 128 - 3 * heads_num
    stat_zeros = jnp.zeros((seq_count, pos_count, stat_pad), jnp.bfloat16)
    query_packed = jnp.concatenate([queries, *split_parts(total_rows, 3), stat_zeros], axis=-1)
    cotangent_free, values_whole = lax.optimization_barrier((cotangent, values_whole))
    cotangent_all = lax.all_gather(cotangent_free, ("ctx", "expert"), axis=0, tiled=True)
    mixer_all = lax.all_gather(mixer_in, "expert", axis=0, tiled=True)
    mixed_heads = attended.reshape(seq_count, pos_count, model_width).astype(jnp.bfloat16)
    hidden_state = residual + jnp.einsum(
        "spd,de->spe", mixed_heads, merge_weight, preferred_element_type=jnp.float32
    )
    second_normed, second_back = jax.vjp(rms_scale, hidden_state, expert_norm_gain)
    expert_input = second_normed.astype(jnp.bfloat16)
    own_hits = jnp.any(
        expert_ids[None] == lax.iota(jnp.int32, expert_num)[:, None, None, None], axis=-1
    )
    own_hot = slot_hot(own_hits, capacity)
    dispatched = (
        jnp.einsum("eskp,spd->eskd", own_hot, expert_input, preferred_element_type=jnp.float32)
        .astype(jnp.bfloat16)
        .reshape(owners, local_experts, lane_rows, model_width)
    )
    arrived = lax.all_to_all(dispatched, "expert", split_axis=0, concat_axis=0, tiled=True)
    slot_rows = arrived.transpose(1, 0, 2, 3).reshape(
        local_experts, owners * lane_rows, model_width
    )
    all_rows = lax.all_gather(slot_rows, "ctx", axis=1, tiled=True)
    my_experts = first_expert + lax.iota(jnp.int32, local_experts)
    block_hits = jnp.any(ids_all[None] == my_experts[:, None, None, None], axis=-1)
    block_hot = slot_hot(block_hits, capacity)
    other_ids = jnp.sum(ids_all, axis=-1)[None] - my_experts[:, None, None]
    row_other = jnp.sum(
        block_hot.astype(jnp.float32) * other_ids[:, :, None, :].astype(jnp.float32), axis=-1
    ).astype(jnp.int32).reshape(local_experts, block_num * capacity)
    cotangent_rows = jnp.einsum(
        "lbkp,bpd->lbkd", block_hot, cotangent_all, preferred_element_type=jnp.float32
    ).astype(jnp.bfloat16).reshape(local_experts, block_num * capacity, model_width)
    row_logits = jnp.einsum(
        "lrd,de->lre", all_rows, router_weight, preferred_element_type=jnp.float32
    )
    expert_line = lax.iota(jnp.int32, expert_num)[None, None, :]
    own_logit = jnp.sum(
        jnp.where(expert_line == my_experts[:, None, None], row_logits, 0.0), axis=-1
    )
    other_logit = jnp.sum(jnp.where(expert_line == row_other[..., None], row_logits, 0.0), axis=-1)
    row_gates = jax.nn.sigmoid(own_logit - other_logit)
    all_grads = (row_gates[..., None] * cotangent_rows.astype(jnp.float32)).astype(jnp.bfloat16)
    gate_pre = jnp.einsum("erd,edf->erf", all_rows, gate_weight, preferred_element_type=jnp.float32)
    up_pre = jnp.einsum("erd,edf->erf", all_rows, up_weight, preferred_element_type=jnp.float32)
    hidden_float, act_back = jax.vjp(gated_hidden, gate_pre, up_pre)
    hidden_act = hidden_float.astype(jnp.bfloat16)
    partial_value = jnp.einsum(
        "erf,efd->erd", hidden_act, down_weight, preferred_element_type=jnp.float32
    ).astype(jnp.bfloat16)
    partial_value, all_grads = lax.optimization_barrier((partial_value, all_grads))
    expert_result = lax.psum_scatter(partial_value, "ctx", scatter_dimension=1, tiled=True)
    returning = expert_result.reshape(local_experts, owners, lane_rows, model_width).transpose(
        1, 0, 2, 3
    )
    returned = lax.all_to_all(returning, "expert", split_axis=0, concat_axis=0, tiled=True)
    hidden_grad = jnp.einsum(
        "erd,efd->erf", all_grads, down_weight, preferred_element_type=jnp.float32
    )
    gate_delta, up_delta = act_back(hidden_grad)
    gate_low = gate_delta.astype(jnp.bfloat16)
    up_low = up_delta.astype(jnp.bfloat16)
    row_part = (
        jnp.einsum("erf,edf->erd", gate_low, gate_weight, preferred_element_type=jnp.float32)
        + jnp.einsum("erf,edf->erd", up_low, up_weight, preferred_element_type=jnp.float32)
    ).astype(jnp.bfloat16)
    row_grads = lax.psum_scatter(row_part, "ctx", scatter_dimension=1, tiled=True)
    back_rows = row_grads.reshape(local_experts, owners, lane_rows, model_width).transpose(
        1, 0, 2, 3
    )
    returned_grads = lax.all_to_all(back_rows, "expert", split_axis=0, concat_axis=0, tiled=True)
    mixed_all = lax.all_gather(mixed_heads, "expert", axis=0, tiled=True)
    query_whole = lax.all_gather(query_packed, ("ctx", "dp"), axis=1, tiled=True)
    down_part = jnp.einsum(
        "erf,erd->efd", hidden_act, all_grads, preferred_element_type=jnp.float32
    )
    gate_part = jnp.einsum("erd,erf->edf", all_rows, gate_low, preferred_element_type=jnp.float32)
    up_part = jnp.einsum("erd,erf->edf", all_rows, up_low, preferred_element_type=jnp.float32)
    gate_grad, up_grad, down_grad = (
        lax.psum_scatter(
            gate_part.astype(jnp.bfloat16), "dp", scatter_dimension=1, tiled=True
        ).astype(jnp.float32),
        lax.psum_scatter(
            up_part.astype(jnp.bfloat16), "dp", scatter_dimension=1, tiled=True
        ).astype(jnp.float32),
        lax.psum_scatter(
            down_part.astype(jnp.bfloat16), "dp", scatter_dimension=2, tiled=True
        ).astype(jnp.float32),
    )
    logits = jnp.einsum(
        "spd,de->spe", expert_input, router_weight, preferred_element_type=jnp.float32
    )
    pick_hot = expert_ids[..., None] == lax.iota(jnp.int32, expert_num)
    picked_logits = jnp.sum(jnp.where(pick_hot, logits[:, :, None, :], 0.0), axis=-1)
    gate_values, gate_back = jax.vjp(pair_softmax, picked_logits)
    upstream = cotangent.astype(jnp.float32)
    slot_table = own_hot.transpose(1, 0, 2, 3)
    choose = (
        slot_table[:, None] * pick_hot.transpose(0, 2, 3, 1)[:, :, :, None, :].astype(jnp.bfloat16)
    ).reshape(seq_count, 2, expert_num * capacity, pos_count)
    returned_rows = returned.reshape(expert_num, seq_count, capacity, model_width).transpose(
        1, 0, 2, 3
    ).reshape(seq_count, expert_num * capacity, model_width)
    picked = jnp.einsum(
        "sjmp,smd->sjpd", choose, returned_rows, preferred_element_type=jnp.float32
    )
    expert_sum = (
        gate_values[:, :, 0, None] * picked[:, 0] + gate_values[:, :, 1, None] * picked[:, 1]
    )
    layer_output = (hidden_state + expert_sum).astype(jnp.bfloat16)
    pair_delta = jnp.sum(upstream[:, None] * picked, axis=-1).transpose(0, 2, 1)
    (pick_grad,) = gate_back(pair_delta)
    logit_grad = jnp.sum(jnp.where(pick_hot, pick_grad[..., None], 0.0), axis=2).astype(
        jnp.bfloat16
    )
    router_part = jnp.einsum(
        "spe,spd->ed", logit_grad, expert_input, preferred_element_type=jnp.float32
    )
    expert_delta = jnp.einsum(
        "spe,de->spd", logit_grad, router_weight, preferred_element_type=jnp.float32
    )
    grad_rows = returned_grads.reshape(expert_num, seq_count, capacity, model_width).transpose(
        1, 0, 2, 3
    ).reshape(seq_count, expert_num * capacity, model_width)
    expert_delta = expert_delta + jnp.einsum(
        "smp,smd->spd",
        slot_table.reshape(seq_count, expert_num * capacity, pos_count),
        grad_rows,
        preferred_element_type=jnp.float32,
    )
    state_part, second_part = second_back(expert_delta)
    state_grad = state_part + upstream
    state_low = state_grad.astype(jnp.bfloat16)
    mixed_flat = jnp.einsum(
        "spe,de->spd", state_low, merge_weight, preferred_element_type=jnp.float32
    ).astype(jnp.bfloat16)
    mixed_grad = mixed_flat.reshape(seq_count, pos_count, heads_num, head_dimension)
    dot_rows = jnp.sum(mixed_grad.astype(jnp.float32) * attended, axis=-1)
    grad_packed = jnp.concatenate([mixed_flat, *split_parts(dot_rows, 3), stat_zeros], axis=-1)
    grad_whole = lax.all_gather(grad_packed, ("ctx", "dp"), axis=1, tiled=True)

    def columns_of(value):
        cut = value.reshape(seq_count, pos_count, owners, column_count).transpose(2, 0, 1, 3)
        return lax.all_to_all(cut, "expert", split_axis=0, concat_axis=0, tiled=True).reshape(
            owners * seq_count, pos_count, column_count
        )

    prob_grad = jnp.einsum(
        "sqhd,skhd->shqk", mixed_grad, value_heads, preferred_element_type=jnp.float32
    )
    row_dot = dot_rows.transpose(0, 2, 1)[..., None]
    score_grad = (prob_mass * (prob_grad - row_dot)).astype(jnp.bfloat16)
    query_back = (
        (
            jnp.einsum("shqk,skhd->sqhd", score_grad, key_heads, preferred_element_type=jnp.float32)
            * score_scale
        )
        .astype(jnp.bfloat16)
        .reshape(seq_count, pos_count, model_width)
    )
    bias_portion = jnp.einsum(
        "stey,aey->at",
        score_grad,
        bucket_table(distance, bucket_num).astype(jnp.bfloat16),
        preferred_element_type=jnp.float32,
    )
    own_keys = keys_local.reshape(seq_count, pos_count, heads_num, head_dimension)
    own_values = values_local.reshape(seq_count, pos_count, heads_num, head_dimension)

    def unpack(packed):
        main = packed[..., :model_width].reshape(seq_count, seq_len, heads_num, head_dimension)
        stat = packed[..., model_width:].astype(jnp.float32)
        joined = (
            stat[..., :heads_num]
            + stat[..., heads_num : 2 * heads_num]
            + stat[..., 2 * heads_num : 3 * heads_num]
        )
        return main, joined.transpose(0, 2, 1)[..., None]

    query_part_heads, total_piece = unpack(query_whole)
    grad_part_heads, dot_piece = unpack(grad_whole)
    gap = lax.iota(jnp.int32, seq_len)[:, None] - query_pos[None, :]
    seen = gap >= 0
    piece_bias = bias_grid(relative_bucket_bias, jnp.clip(gap, 0, seq_len - 1))
    raw_piece = (
        jnp.einsum(
            "sqhd,skhd->shqk", query_part_heads, own_keys, preferred_element_type=jnp.float32
        )
        * score_scale
        + piece_bias[None]
    )
    prob_piece = jnp.exp(jnp.where(seen[None, None], raw_piece, -1e30) - total_piece)
    grad_prob = jnp.einsum(
        "sqhd,skhd->shqk", grad_part_heads, own_values, preferred_element_type=jnp.float32
    )
    score_piece = (prob_piece * (grad_prob - dot_piece)).astype(jnp.bfloat16)
    key_back = (
        (
            jnp.einsum(
                "shqk,sqhd->skhd", score_piece, query_part_heads, preferred_element_type=jnp.float32
            )
            * score_scale
        )
        .astype(jnp.bfloat16)
        .reshape(seq_count, pos_count, model_width)
    )
    value_back = (
        jnp.einsum(
            "shqk,sqhd->skhd",
            prob_piece.astype(jnp.bfloat16),
            grad_part_heads,
            preferred_element_type=jnp.float32,
        )
        .astype(jnp.bfloat16)
        .reshape(seq_count, pos_count, model_width)
    )
    merge_part = jnp.einsum(
        "spd,spc->dc", mixed_all, columns_of(state_low), preferred_element_type=jnp.float32
    ).astype(jnp.bfloat16)
    merge_sum = lax.psum_scatter(
        merge_part, ("ctx", "dp"), scatter_dimension=0, tiled=True
    ).astype(jnp.float32)
    back_cut = jnp.stack(
        [
            part.reshape(seq_count, pos_count, owners, column_count).transpose(2, 0, 1, 3)
            for part in (query_back, key_back, value_back)
        ],
        axis=1,
    )
    back_all = lax.all_to_all(back_cut, "expert", split_axis=0, concat_axis=0, tiled=True)
    back_part = (
        jnp.einsum(
            "ospd,onspc->dnc",
            mixer_all.reshape(owners, seq_count, pos_count, model_width),
            back_all,
            preferred_element_type=jnp.float32,
        )
        .reshape(model_width, 3 * column_count)
        .astype(jnp.bfloat16)
    )
    back_sum = lax.psum_scatter(
        back_part, ("ctx", "dp"), scatter_dimension=0, tiled=True
    ).astype(jnp.float32)
    mixer_delta = jnp.einsum(
        "spe,de->spd", query_back, query_weight, preferred_element_type=jnp.float32
    )
    mixer_delta = mixer_delta + jnp.einsum(
        "spe,de->spd", key_back, key_weight, preferred_element_type=jnp.float32
    )
    mixer_delta = mixer_delta + jnp.einsum(
        "spe,de->spd", value_back, value_weight, preferred_element_type=jnp.float32
    )
    input_part, first_part = first_back(mixer_delta)
    input_grad = state_grad + input_part
    second_sum, router_sum = total_over((second_part, router_part), everyone)
    first_sum, bias_total = total_over((first_part, bias_portion), everyone)
    return (
        layer_output,
        input_grad,
        first_sum,
        back_sum[:, :column_count],
        back_sum[:, column_count : 2 * column_count],
        back_sum[:, 2 * column_count :],
        merge_sum,
        bias_total,
        second_sum,
        router_sum.T,
        gate_grad,
        up_grad,
        down_grad,
    )


def solution(mesh):
    in_specs = (
        P("expert", ("ctx", "dp"), None),
        P("expert", ("ctx", "dp"), None),
        P("expert", ("ctx", "dp"), None),
        P(),
        P(),
        P(),
        P(),
        P(),
        P(),
        P(),
        P(),
        P("expert", None, "ctx"),
        P("expert", None, "ctx"),
        P("expert", "ctx", None),
    )
    out_specs = (
        P("expert", ("ctx", "dp"), None),
        P("expert", ("ctx", "dp"), None),
        P(),
        P(("ctx", "dp"), "expert"),
        P(("ctx", "dp"), "expert"),
        P(("ctx", "dp"), "expert"),
        P(("ctx", "dp"), "expert"),
        P(),
        P(),
        P(),
        P("expert", "dp", "ctx"),
        P("expert", "dp", "ctx"),
        P("expert", "ctx", "dp"),
    )
    return jax.shard_map(
        per_device, mesh=mesh, in_specs=in_specs, out_specs=out_specs, check_vma=False
    )
```

time: 568 us -> 565 us (level)
  waiting for transfers between devices: 217 us -> 66.7 us
  blocking collectives: 99.8 us -> 226 us
  matrix products: 118 us -> 141 us
  local copies, waits for them, and re-layouts: 61.3 us -> 45.8 us
  other arithmetic: 38.6 us -> 46.4 us
  starting transfers between devices: 10.6 us -> 17.7 us
    all_gather x2 -> x5, blocking collectives: 28.9 us -> 201 us  [the longest x2 136 us: total_over(): lax.all_gather(packed, axes, axis=0, tiled=True)]
    reduce_scatter x1 -> x2, waiting for transfers between devices: 97.1 us -> 33.2 us  [the longest x1 33.2 us: per_device(): lax.psum_scatter(merge_part, ('ctx', 'dp'), scatter_dimension=0, tiled=True)]
    psum x1 -> x0, blocking collectives: 37.8 us -> none  [per_device(): lax.psum((first_part, second_part, router_part, bias_portion), ('expert',...]
    reduce_scatter x1, waiting for transfers between devices: 36.5 us -> 0.02 us  [per_device(): lax.psum_scatter(partial_value, 'ctx', scatter_dimension=1, tiled=True)]
    reduce_scatter x1, waiting for transfers between devices: 35.7 us -> 0.02 us  [per_device(): lax.psum_scatter(row_part, 'ctx', scatter_dimension=1, tiled=True)]
    dot_general x11 -> x16, matrix products: 36.6 us -> 61.6 us  [the longest x2 31.5 us: bias_grid(): jnp.einsum('ry,rta->yta', table, jnp.concatenate([hot, hot, hot], axis=0)...]
    all_to_all x1 -> x0, blocking collectives: 15.4 us -> none  [per_device(): lax.all_to_all(grad_slots, 'expert', split_axis=0, concat_axis=0, tiled=T...]
    all_gather x3, waiting for transfers between devices: 13.4 us -> 0.04 us  [the longest x1 0.02 us: per_device(): grad_whole = lax.all_gather(grad_packed, ('ctx', 'dp'), axis=1, tiled=True)]
  transfers between devices with their start and end apart: 14 -> 17, of which waited for: 7 -> 4; matrix products, arithmetic and copies ran while one was open for 32% -> 39% of each run, Pallas kernels for 0% -> 0%
where the time goes in v1:
time: 565 us; the launch traced here: 559 us
  blocking collectives  226 us (40%)
  matrix products  141 us (25%)
  waiting for transfers between devices  66.7 us (12%)
  other arithmetic  46.4 us (8%)
  local copies, waits for them, and re-layouts  45.8 us (8%)
  starting transfers between devices  17.7 us (3%)
  between operations  15.4 us (3%)
    all_gather x2, blocking collectives, total_over(): lax.all_gather(packed, axes, axis=0, tiled=True)  136 us
    reduce_scatter x1, waiting for transfers between devices, per_device(): lax.psum_scatter(merge_part, ('ctx', 'dp'), scatter_dimension=0, tiled=True)  33.2 us
    dot_general x2, matrix products, bias_grid(): jnp.einsum('ry,rta->yta', table, jnp.concatenate([hot, hot, hot], axis=0)...  31.5 us
    all_gather x1, blocking collectives, per_device(): ids_all = lax.all_gather(expert_ids, ('ctx', 'expert'), axis=0, tiled=True)  29.1 us
    all_gather x1, waiting for transfers between devices, per_device(): lax.all_gather(values_local, ('ctx', 'dp'), axis=1, tiled=True)  25.7 us
    all_to_all x1, blocking collectives, per_device(): lax.all_to_all(dispatched, 'expert', split_axis=0, concat_axis=0, tiled=T...  24.2 us
    unnamed x163, local copies, waits for them, and re-layouts  19.7 us
    all_gather x1, blocking collectives, per_device(): mixer_all = lax.all_gather(mixer_in, 'expert', axis=0, tiled=True)  18.5 us
  transfers between devices with their start and end apart: 17, of which 4 were waited for; matrix products, arithmetic and copies ran while one was open for 39% of the time, Pallas kernels for 0%

profile of v1, /device:TPU:0, one launch (start us, length us, event | category | flops | bytes accessed | tf_op | source)
XLA Modules:
  0.0 558.6 jit_solution(17168652292578200525)
XLA Ops:
  18.9 6.5 %convert_convert_fusion.1 = bf16[32,128,1024]{2,0,1:T(8,128)(2,1)} fusion(s32[128,1024]{1,0:T(8,128)S(1)} %convert_add_fusion.1), kind=kLoop, calls=%fused_computation.14 | loop fusion | flops 12582912 | bytes 8912896 | tf_op jit(solution)/shard_map/convert_element_type | solution.py:65
  25.5 15.7 %fusion = f32[12,128,1024]{2,0,1:T(8,128)} fusion(bf16[32,128,1024]{2,0,1:T(8,128)(2,1)} %convert_convert_fusion.1, bf16[32,12]{0,1:T(8,128)(2,1)S(1)} %get-tuple-element.91, bf16[32,12]{0,1:T(8,128)(2,1)S(1)} %get-tuple-element.92, bf16[32,12]{0,1:T(8,128)(2,1)S(1)} %get-tuple-element.90), kind=kOutput, calls=%fused_computation | convolution fusion | flops 377494272 | bytes 14682368 | tf_op jit(solution)/shard_map/ry,rta->yta/dot_general | solution.py:67
  42.9 25.7 %all-gather.17.cloned.1.call-done = bf16[1024,768]{1,0:T(8,128)(2,1)} async-done(((bf16[128,768]{1,0:T(8,128)(2,1)}), bf16[1024,768]{1,0:T(8,128)(2,1)}) %all-gather.17.cloned.1.call-update) | async-done | bytes 1572880 | tf_op jit(solution)/shard_map/all_gather | solution.py:146
  71.2 8.2 %fusion.228 = (f32[12,128]{1,0:T(8,128)S(1)}, f32[12,128,1024]{2,1,0:T(8,128)S(1)}) fusion(f32[12,128,1024]{2,0,1:T(8,128)} %fusion, bf16[128,12,64]{0,2,1:T(8,128)(2,1)S(1)} %bitcast.395, bf16[1024,12,64]{0,2,1:T(8,128)(2,1)S(1)} %bitcast.374, pred[128,1024]{1,0:T(8,128)(4,1)S(1)} %copy-done.33), kind=kOutput, calls=%fused_computation.329 | convolution fusion | flops 207616512 | bytes 14489600 | tf_op jit(solution)/shard_map/sqhd,skhd->shqk/dot_general | solution.py:161
  85.9 24.2 %all_to_all.25 = bf16[4,1,72,768]{3,2,1,0:T(8,128)(2,1)} all-to-all(bf16[4,1,72,768]{3,2,1,0:T(8,128)(2,1)S(1)} %fusion.72), channel_id=1, replica_groups=mesh['expert'=4,'ctx'=4,'dp'=2] {'expert'}, dimensions={0} | all-to-all | bytes 884736 | tf_op jit(solution)/shard_map/all_to_all | solution.py:199
  110.2 29.1 %all_gather.36 = s32[16,128,2]{1,2,0:T(2,128)S(1)} all-gather(s32[1,128,2]{1,2,0:T(2,128)S(1)} %copy-done.46), channel_id=1, replica_groups=mesh['expert'=4,'ctx'=4,'dp'=2] {'ctx','expert'}, dimensions={0}, use_global_device_ids=true | all-gather | bytes 17408 | tf_op jit(solution)/shard_map/all_gather | solution.py:133
  151.3 10.5 %multiply_convert_fusion.3 = (bf16[1152,768]{1,0:T(8,128)(2,1)S(1)}, f32[1152,768]{1,0:T(8,128)}, f32[1152,768]{1,0:T(8,128)}) fusion(f32[1152,768]{1,0:T(8,128)S(1)} %fusion.51, bf16[1,768,768]{2,1,0:T(8,128)(2,1)S(1)} %copy-done, bf16[1,1152,768]{2,1,0:T(8,128)(2,1)S(1)} %copy-done.20), kind=kOutput, calls=%fused_computation.36 | convolution fusion | flops 1417347072 | bytes 15335424 | tf_op jit(solution)/shard_map/erd,edf->erf/dot_general | solution.py:225
  169.0 7.7 %multiply_convert_fusion.2 = (bf16[1152,768]{1,0:T(8,128)(2,1)S(1)}, bf16[1152,768]{1,0:T(8,128)(2,1)S(1)}) fusion(f32[1152,768]{1,0:T(8,128)} %get-tuple-element.78, f32[1152,768]{1,0:T(8,128)} %copy-done.73, f32[1152,768]{1,0:T(8,128)} %get-tuple-element.103, bf16[1,768,768]{2,1,0:T(8,128)(2,1)} %param.27, bf16[1,1152,768]{2,1,0:T(8,128)(2,1)} %fusion.21), kind=kOutput, calls=%fused_computation.34 | convolution fusion | flops 1374879744 | bytes 17104896 | tf_op jit(solution)/shard_map/erd,efd->erf/dot_general | solution.py:237
  185.0 5.1 convert_convert_fusion
  191.9 4.5 copy.164
  200.9 15.8 %fusion.6 = f32[12,1024,128]{2,0,1:T(8,128)} fusion(bf16[32,1024,128]{2,0,1:T(8,128)(2,1)} %convert_convert_fusion, bf16[32,12]{0,1:T(8,128)(2,1)S(1)} %copy-done.64, bf16[32,12]{0,1:T(8,128)(2,1)S(1)} %copy-done.66, bf16[32,12]{0,1:T(8,128)(2,1)S(1)} %copy-done.62), kind=kOutput, calls=%fused_computation.6 | convolution fusion | flops 377494272 | bytes 14682368 | tf_op jit(solution)/shard_map/ry,rta->yta/dot_general | solution.py:67
  220.4 18.5 %all_gather.41 = bf16[4,128,768]{2,1,0:T(8,128)(2,1)} all-gather(bf16[1,128,768]{2,1,0:T(8,128)(2,1)S(1)} %fusion.166), channel_id=1, replica_groups=mesh['expert'=4,'ctx'=4,'dp'=2] {'expert'}, dimensions={0}, use_global_device_ids=true | all-gather | bytes 983040 | tf_op jit(solution)/shard_map/all_gather | solution.py:183
  239.9 18.1 %all_gather.42 = bf16[4,128,768]{2,1,0:T(8,128)(2,1)} all-gather(bf16[1,128,768]{2,1,0:T(8,128)(2,1)S(1)} %copy.155), channel_id=1, replica_groups=mesh['expert'=4,'ctx'=4,'dp'=2] {'expert'}, dimensions={0}, use_global_device_ids=true | all-gather | bytes 983040 | tf_op jit(solution)/shard_map/all_gather | solution.py:252
  263.4 4.1 all-to-all-start.1
  269.0 4.8 fusion.65
  277.0 4.1 all-to-all-start.2
  300.2 9.1 %fusion.14 = f32[12,1024,128]{2,1,0:T(8,128)} fusion(f32[12,1024,128]{2,0,1:T(8,128)} %fusion.6, f32[12,1024]{1,0:T(8,128)} %copy.145, pred[1024,128]{1,0:T(8,128)(4,1)} %fusion.98, bf16[1024,12,64]{0,2,1:T(8,128)(2,1)S(1)} %bitcast.372, bf16[128,12,64]{0,2,1:T(8,128)(2,1)} %bitcast.394), kind=kOutput, calls=%fused_computation.19 | convolution fusion | flops 207618048 | bytes 14532608 | tf_op jit(solution)/shard_map/sqhd,skhd->shqk/dot_general | solution.py:366
  321.4 4.5 multiply_convert_fusion.1
  332.0 4.0 all-to-all-start.4
  336.1 67.4 %all_gather.43 = f32[32,32,128]{2,1,0:T(8,128)S(1)} all-gather(f32[1,32,128]{2,1,0:T(8,128)S(1)} %fusion.200), channel_id=1, replica_groups=mesh['expert'=4,'ctx'=4,'dp'=2] {'expert','ctx','dp'}, dimensions={0}, use_global_device_ids=true | all-gather | bytes 540672 | tf_op jit(solution)/shard_map/all_gather | solution.py:94
  414.6 6.8 %fusion.85 = bf16[12,64,128]{2,1,0:T(8,128)(2,1)} fusion(bf16[1024,12,64]{0,2,1:T(8,128)(2,1)S(1)} %bitcast.373, f32[12,1024,128]{2,1,0:T(8,128)} %fusion.14, f32[12,1024]{1,0:T(8,128)S(1)} %copy.151, bf16[1024,12,64]{0,2,1:T(8,128)(2,1)} %bitcast.376, bf16[128,12,64]{0,2,1:T(8,128)(2,1)S(1)} %bitcast.398), kind=kOutput, calls=%fused_computation.106 | convolution fusion | flops 407568384 | bytes 9879552 | tf_op jit(solution)/shard_map/shqk,sqhd->skhd/dot_general | solution.py:379
  426.8 4.2 all-to-all-start.3
  435.9 33.2 %reduce-scatter.16.cloned.1.call-done = bf16[96,192]{1,0:T(8,128)(2,1)} async-done(((bf16[768,192]{1,0:T(8,128)(2,1)}), bf16[96,192]{1,0:T(8,128)(2,1)}) %reduce-scatter.16.cloned.1.call-update) | async-done | bytes 36880 | tf_op jit(solution)/shard_map/reduce_scatter | solution.py:400
  477.5 68.2 %all_gather.40 = f32[32,16,128]{2,1,0:T(8,128)S(1)} all-gather(f32[1,16,128]{2,1,0:T(8,128)S(1)} %fusion.201), channel_id=1, replica_groups=mesh['expert'=4,'ctx'=4,'dp'=2] {'expert','ctx','dp'}, dimensions={0}, use_global_device_ids=true | all-gather | bytes 270336 | tf_op jit(solution)/shard_map/all_gather | solution.py:94
  (323 shorter events, 143.2 us)
Async XLA Ops:
  7.2 144.1 %copy-start = (bf16[1,768,768]{2,1,0:T(8,128)(2,1)S(1)}, bf16[1,768,768]{2,1,0:T(8,128)(2,1)}, u32[]{:S(2)}) copy-start(bf16[1,768,768]{2,1,0:T(8,128)(2,1)} %param.26) | copy-start | bytes 3538948
  7.2 34.0 %all-gather.19.cloned.1.call-start = ((), (), s32[]{:S(2)}) async-start(), calls=%async_computation.23 | async-start | bytes 1769472 | tf_op jit(solution)/shard_map/all_gather | solution.py:145
  11.8 56.8 %all-gather.17.cloned.1.call-start = ((), (), s32[]{:S(2)}) async-start(), calls=%async_computation.22 | async-start | bytes 1769472 | tf_op jit(solution)/shard_map/all_gather | solution.py:146
  14.2 127.6 %all-gather.11.cloned.1.call-start = ((), (), s32[]{:S(2)}) async-start(), calls=%async_computation.13 | async-start | bytes 3342336 | tf_op jit(solution)/shard_map/all_gather | solution.py:182
  14.9 130.6 %all-gather.9.cloned.1.call-start = ((), (), s32[]{:S(2)}) async-start(), calls=%async_computation.12 | async-start | bytes 2211840 | tf_op jit(solution)/shard_map/all_gather | solution.py:203
  85.7 153.4 %copy-start.13 = (bf16[1,128,768]{2,1,0:T(8,128)(2,1)}, bf16[1,128,768]{2,1,0:T(8,128)(2,1)S(1)}, u32[]{:S(2)}) copy-start(bf16[1,128,768]{2,1,0:T(8,128)(2,1)S(1)} %multiply_convert_fusion.9) | copy-start | bytes 589828
  110.2 147.8 %all-gather.13.cloned.1.call-start = ((), (), s32[]{:S(2)}) async-start(), calls=%async_computation.16 | async-start | bytes 2064384 | tf_op jit(solution)/shard_map/all_gather | solution.py:253
  141.3 122.1 %reduce-scatter.10.cloned.1.call-start = ((), (), s32[]{:S(2)}) async-start(), calls=%async_computation.14 | async-start | bytes 2211840 | tf_op jit(solution)/shard_map/reduce_scatter | solution.py:232
  168.9 104.9 %reduce-scatter.12.cloned.1.call-start = ((), (), s32[]{:S(2)}) async-start(), calls=%async_computation.15 | async-start | bytes 2211840 | tf_op jit(solution)/shard_map/reduce_scatter | solution.py:247
  181.4 127.9 %reduce-scatter.22.cloned.1.call-start = ((), (), s32[]{:S(2)}) async-start(), calls=%async_computation.24 | async-start | bytes 1769472
  199.4 116.7 %reduce-scatter.18.cloned.1.call-start = ((), (), s32[]{:S(2)}) async-start(), calls=%async_computation.20 | async-start | bytes 1769472 | tf_op jit(solution)/shard_map/reduce_scatter | solution.py:260
  263.4 13.6 %all-to-all-start.1 = ((bf16[4,1,72,768]{3,2,1,0:T(8,128)(2,1)}), bf16[4,1,72,768]{3,2,1,0:T(8,128)(2,1)}, u32[]{:S(2)}, u32[]{:S(2)}) async-start(bf16[4,1,72,768]{3,2,1,0:T(8,128)(2,1)} %bitcast.401), calls=%async_computation.2 | async-start | bytes 884736 | tf_op jit(solution)/shard_map/all_to_all | solution.py:236
  267.6 50.7 %reduce-scatter.20.cloned.1.call-start = ((), (), s32[]{:S(2)}) async-start(), calls=%async_computation.21 | async-start | bytes 1769472 | tf_op jit(solution)/shard_map/reduce_scatter | solution.py:263
  277.0 13.6 %all-to-all-start.2 = ((bf16[4,1,72,768]{3,2,1,0:T(8,128)(2,1)}), bf16[4,1,72,768]{3,2,1,0:T(8,128)(2,1)}, u32[]{:S(2)}, u32[]{:S(2)}) async-start(bf16[4,1,72,768]{3,2,1,0:T(8,128)(2,1)} %bitcast.400), calls=%async_computation.4 | async-start | bytes 884736 | tf_op jit(solution)/shard_map/all_to_all | solution.py:251
  281.2 126.6 %all-gather.15.cloned.1.call-start = ((), (), s32[]{:S(2)}) async-start(), calls=%async_computation.17 | async-start | bytes 2064384 | tf_op jit(solution)/shard_map/all_gather | solution.py:320
  332.0 94.9 %all-to-all-start.4 = ((bf16[4,1,128,192]{2,3,1,0:T(8,128)(2,1)}), bf16[4,1,128,192]{2,3,1,0:T(8,128)(2,1)}, u32[]{:S(2)}, u32[]{:S(2)}) async-start(bf16[4,1,128,192]{2,3,1,0:T(8,128)(2,1)} %bitcast.106), calls=%async_computation.7 | async-start | bytes 393216 | tf_op jit(solution)/shard_map/all_to_all | solution.py:324
  426.8 43.8 %all-to-all-start.3 = ((bf16[4,3,1,128,192]{3,4,2,1,0:T(8,128)(2,1)}), bf16[4,3,1,128,192]{3,4,2,1,0:T(8,128)(2,1)}, u32[]{:S(2)}, u32[]{:S(2)}) async-start(bf16[4,3,1,128,192]{3,4,2,1,0:T(8,128)(2,1)} %pad_maximum_fusion), calls=%async_computation.5 | async-start | bytes 1179648 | tf_op jit(solution)/shard_map/all_to_all | solution.py:410
  431.0 38.1 %reduce-scatter.16.cloned.1.call-start = ((), (), s32[]{:S(2)}) async-start(), calls=%async_computation.19 | async-start | bytes 442368 | tf_op jit(solution)/shard_map/reduce_scatter | solution.py:400
  434.1 115.9 %reduce-scatter.14.cloned.1.call-start = ((), (), s32[]{:S(2)}) async-start(), calls=%async_computation.18 | async-start | bytes 1105920 | tf_op jit(solution)/shard_map/reduce_scatter | solution.py:421
  473.7 74.0 %copy-start.11 = (f32[128,768]{1,0:T(8,128)S(1)}, f32[128,768]{1,0:T(8,128)}, u32[]{:S(2)}) copy-start(f32[128,768]{1,0:T(8,128)} %copy-done.10) | copy-start | bytes 1179652
  473.7 74.0 %copy-start.17 = (bf16[1,128,768]{2,1,0:T(8,128)(2,1)S(1)}, bf16[1,128,768]{2,1,0:T(8,128)(2,1)}, u32[]{:S(2)}) copy-start(bf16[1,128,768]{2,1,0:T(8,128)(2,1)} %param.15) | copy-start | bytes 589828
  473.7 74.0 %copy-start.38 = (f32[768]{0:T(1024)S(1)}, f32[768]{0:T(1024)}, u32[]{:S(2)}) copy-start(f32[768]{0:T(1024)} %param.23) | copy-start | bytes 9220
  473.7 74.0 %copy-start.56 = (f32[128]{0:T(128)S(1)}, f32[128]{0:T(128)}, u32[]{:S(2)}) copy-start(f32[128]{0:T(128)} %copy-done.55) | copy-start | bytes 1540
  473.7 77.8 %copy-start.1 = (bf16[1,768,768]{2,1,0:T(8,128)(2,1)S(1)}, bf16[1,768,768]{2,1,0:T(8,128)(2,1)}, u32[]{:S(2)}) copy-start(bf16[1,768,768]{2,1,0:T(8,128)(2,1)} %param.26) | copy-start | bytes 3538948
  (72 other events, 795.3 us)
Sparse Core Ops, SparseCore 0:
  12.0 28.3 all-gather.18
  42.8 25.7 all-gather.16
  70.9 46.8 all-gather.10
  119.3 19.2 all-gather.8
  141.4 25.6 all-gather.12
  169.6 29.3 reduce-scatter.9
  201.7 29.3 reduce-scatter.11
  233.9 21.7 reduce-scatter.21
  258.6 21.7 reduce-scatter.17
  282.5 21.7 reduce-scatter.19
  306.9 26.8 all-gather.14
  434.9 34.2 reduce-scatter.15
  473.9 35.9 reduce-scatter.13
